TPU v7x, 32 devices: a whole 2x2x4 slice. The times are simulated.
32 devices in a mesh: gx: 4 (over y, core), gy: 4 (over z), gz: 2 (over x).
Axes of the slice: x: 2, y: 2, z: 4, core: 2. Of those that a mesh axis runs over, the one named last changes fastest.
Arguments:
- concentration: float32 [192, 64, 256], P('gx', 'gy', 'gz'), may hold values from -6 to 6
- dispersion: float32 [192, 64, 256], P('gx', 'gy', 'gz'), may hold values from 0.2 to 1.2
- disp_step: float32 [192, 64, 256], P('gx', 'gy', 'gz'), may hold values from -6 to 6
- capacity: float32 [192, 64, 256], P('gx', 'gy', 'gz'), may hold values from 1 to 4
- cap_step: float32 [192, 64, 256], P('gx', 'gy', 'gz'), may hold values from -6 to 6
- velocity: float32 [192, 64, 256], P('gx', 'gy', 'gz'), may hold values from 0.2 to 1
- voxel_mask: int32 [24, 8, 32], P('gx', 'gy', 'gz'), may hold values 0 or 1
- voxel_class: int32 [24, 8, 32], P('gx', 'gy', 'gz'), may hold values from 0 to 3
- class_weight: float32 [4], replicated, may hold values from 4 to 40
Outputs:
- grad_dispersion: float32 [192, 64, 256], P('gx', 'gy', 'gz')
- grad_capacity: float32 [192, 64, 256], P('gx', 'gy', 'gz')
All inputs are finite; a program needn't handle non-finite values. No bound on the sum of `voxel_mask` on one device may be relied on, other than what follows from the above.
Results may differ from a plain program's by a relative error of at most 0.00024.
Values sent between devices are 32-bit elements; how exact they have to be, the bound alone decides.
A program may use at most 64 MiB of HBM per device.

v0:
```python
import jax
import jax.numpy as jnp
from jax import lax
from jax.sharding import PartitionSpec as P

time_step = 0.1


def extended(x, sides, width):
    for axis, dim in sides:
        size, length = (lax.axis_size(axis), x.shape[dim])
        up = [(i, (i + 1) % size) for i in range(size - 1)]
        down = [(j, i) for i, j in up]
        last = lax.slice_in_dim(x, length - width, length, axis=dim)
        leading = lax.slice_in_dim(x, 0, width, axis=dim)
        before = lax.ppermute(last, axis, up)
        after = lax.ppermute(leading, axis, down)
        x = jnp.concatenate([before, x, after], axis=dim)
    return x


def sides(padded):
    return [
        padded[2:, 1:-1, 1:-1],
        padded[:-2, 1:-1, 1:-1],
        padded[1:-1, 2:, 1:-1],
        padded[1:-1, :-2, 1:-1],
        padded[1:-1, 1:-1, 2:],
        padded[1:-1, 1:-1, :-2],
    ]


def inner(padded):
    return padded[1:-1, 1:-1, 1:-1]


def diffuse(field_pad, coef_pad):
    center = inner(field_pad)
    coef = inner(coef_pad)
    total = jnp.zeros(center.shape, jnp.float32)
    for near_field, near_coef in zip(sides(field_pad), sides(coef_pad)):
        total = total + 0.5 * (coef + near_coef) * (near_field - center)
    return total


def advect(field_pad, vel_pad):
    return vel_pad[1:-1, 1:-1, :-2] * field_pad[1:-1, 1:-1, :-2] - inner(vel_pad) * inner(field_pad)


def advect_back(field_pad, vel_center):
    return vel_center * (field_pad[1:-1, 1:-1, 2:] - inner(field_pad))


def face_grad(mult_pad, field_pad):
    mult = inner(mult_pad)
    center = inner(field_pad)
    total = jnp.zeros(center.shape, jnp.float32)
    for near_mult, near_field in zip(sides(mult_pad), sides(field_pad)):
        total = total + 0.5 * (mult - near_mult) * (near_field - center)
    return total


def voxel_weights(voxel_mask, voxel_class, class_weight):
    labels = jnp.arange(class_weight.shape[0])
    picked = jnp.where(
        voxel_class[None] == labels[:, None, None, None], class_weight[:, None, None, None], 0.0
    )
    return voxel_mask.astype(jnp.float32) * jnp.sum(picked, axis=0)


def restrict_value(final, weights):
    sx, sy, sz = weights.shape
    coarse = final.reshape(sx, 8, sy, 8, sz, 8).mean(axis=(1, 3, 5))
    return weights * coarse


def prolong(valued):
    sx, sy, sz = valued.shape
    return jnp.broadcast_to(valued[:, None, :, None, :, None], (sx, 8, sy, 8, sz, 8)).reshape(
        sx * 8, sy * 8, sz * 8
    )


def inside_line(position, count, local, depth):
    start = position * local - depth
    where_at = start + jnp.arange(local + 2 * depth)
    return (where_at >= 0) & (where_at < local * count)


def inside_box(extent_x, extent_y, extent_z, depth):
    line_x = inside_line(lax.axis_index("gx"), lax.axis_size("gx"), extent_x, depth)
    line_y = inside_line(lax.axis_index("gy"), lax.axis_size("gy"), extent_y, depth)
    line_z = inside_line(lax.axis_index("gz"), lax.axis_size("gz"), extent_z, depth)
    return line_x[:, None, None] & line_y[None, :, None] & line_z[None, None, :]


def shards(
    concentration,
    dispersion,
    disp_step,
    capacity,
    cap_step,
    velocity,
    voxel_mask,
    voxel_class,
    class_weight,
):
    extent_x, extent_y, extent_z = concentration.shape
    stacked = jnp.stack([concentration, dispersion, disp_step, velocity, capacity, cap_step])
    wide = extended(stacked, (("gx", 1), ("gy", 2), ("gz", 3)), 2)
    conc_wide = wide[0]
    disp_wide = wide[1]
    step_wide = wide[2]
    vel_wide = wide[3]
    inside = inside_box(extent_x, extent_y, extent_z, 1)
    cap_ext = jnp.where(inside, inner(wide[4]), 1.0)
    capstep_ext = inner(wide[5])
    rate_ext = diffuse(conc_wide, disp_wide) + advect(conc_wide, vel_wide)
    conc_pad = inner(conc_wide)
    disp_pad = inner(disp_wide)
    step_pad = inner(step_wide)
    vel_pad = inner(vel_wide)
    later_pad = jnp.where(inside, conc_pad + time_step / cap_ext * rate_ext, 0.0)
    tangent_pad = jnp.where(
        inside,
        time_step / cap_ext * diffuse(conc_wide, step_wide)
        - time_step * capstep_ext / cap_ext**2 * rate_ext,
        0.0,
    )
    first_rate = inner(rate_ext)
    second_rate = diffuse(later_pad, disp_pad) + advect(later_pad, vel_pad)
    final = (
        inner(tangent_pad)
        + time_step
        / capacity
        * (
            diffuse(tangent_pad, disp_pad)
            + advect(tangent_pad, vel_pad)
            + diffuse(later_pad, step_pad)
        )
        - time_step * cap_step / capacity**2 * second_rate
    )
    weights = voxel_weights(voxel_mask, voxel_class, class_weight)
    valued = restrict_value(final, weights)
    source = prolong(valued)
    scaled = time_step * source / capacity
    scaled_pad = extended(scaled, (("gx", 0), ("gy", 1), ("gz", 2)), 1)
    earlier = source + diffuse(scaled_pad, disp_pad) + advect_back(scaled_pad, velocity)
    scaled_first = time_step * earlier / capacity
    first_pad = extended(scaled_first, (("gx", 0), ("gy", 1), ("gz", 2)), 1)
    grad_dispersion = face_grad(scaled_pad, later_pad) + face_grad(first_pad, conc_pad)
    grad_capacity = -scaled * second_rate / capacity - scaled_first * first_rate / capacity
    return (grad_dispersion, grad_capacity)


def solution(mesh):
    in_specs = (
        P("gx", "gy", "gz"),
        P("gx", "gy", "gz"),
        P("gx", "gy", "gz"),
        P("gx", "gy", "gz"),
        P("gx", "gy", "gz"),
        P("gx", "gy", "gz"),
        P("gx", "gy", "gz"),
        P("gx", "gy", "gz"),
        P(),
    )
    out_specs = (P("gx", "gy", "gz"), P("gx", "gy", "gz"))
    return jax.shard_map(shards, mesh=mesh, in_specs=in_specs, out_specs=out_specs, check_vma=False)
```

profile of v0, /device:TPU:22, one launch (start us, length us, event | category | flops | bytes accessed | tf_op | source)
XLA Modules:
  0.0 159.4 jit_solution(412401229279034234)
XLA Ops:
  0.7 1.1 bitcast_dynamic-update-slice_fusion.5
  1.8 1.1 bitcast_dynamic-update-slice_fusion.4
  3.0 0.8 copy-done.4
  3.9 1.9 %collective-permute-start = (f32[6,2,16,128]{3,2,1,0:T(8,128)S(1)}, f32[6,2,16,128]{3,2,1,0:T(8,128)S(1)}, u32[]{:S(2)}, u32[]{:S(2)}) collective-permute-start(f32[6,2,16,128]{3,2,1,0:T(8,128)S(1)} %get-tuple-element.18), channel_id=1, source_target_pairs={{0,8},{8,16},{16,24},{1,9},{9,17},{17,25},{2,10},{10,18},{18,26},{... | collective-permute-start | bytes 294920 | tf_op jit(solution)/shard_map/ppermute | solution.py:16
  5.8 3.6 %collective-permute-start.1 = (f32[6,2,16,128]{3,2,1,0:T(8,128)S(1)}, f32[6,2,16,128]{3,2,1,0:T(8,128)S(1)}, u32[]{:S(2)}, u32[]{:S(2)}) collective-permute-start(f32[6,2,16,128]{3,2,1,0:T(8,128)S(1)} %get-tuple-element.19), channel_id=1, source_target_pairs={{8,0},{16,8},{24,16},{9,1},{17,9},{25,17},{10,2},{18,10},{26,18},{... | collective-permute-start | bytes 294920 | tf_op jit(solution)/shard_map/ppermute | solution.py:17
  9.5 0.1 select_reduce_fusion
  9.6 0.2 collective-permute-done
  9.8 1.8 %collective-permute-done.1 = f32[6,2,16,128]{3,2,1,0:T(8,128)S(1)} collective-permute-done((f32[6,2,16,128]{3,2,1,0:T(8,128)S(1)}, f32[6,2,16,128]{3,2,1,0:T(8,128)S(1)}, u32[]{:S(2)}, u32[]{:S(2)}) %collective-permute-start.1) | collective-permute-done | bytes 98336 | tf_op jit(solution)/shard_map/ppermute | solution.py:17
  11.7 0.2 pad_maximum_fusion.42
  11.9 3.5 %collective-permute-start.2 = (f32[6,52,2,128]{3,2,1,0:T(2,128)S(1)}, f32[6,52,2,128]{3,2,1,0:T(2,128)S(1)}, u32[]{:S(2)}, u32[]{:S(2)}) collective-permute-start(f32[6,52,2,128]{3,2,1,0:T(2,128)S(1)} %get-tuple-element.16), channel_id=1, source_target_pairs={{0,2},{2,4},{4,6},{1,3},{3,5},{5,7},{8,10},{10,12},{12,14},{9,11},... | collective-permute-start | bytes 958472 | tf_op jit(solution)/shard_map/ppermute | solution.py:16
  15.4 2.4 %collective-permute-start.3 = (f32[6,52,2,128]{3,2,1,0:T(2,128)S(1)}, f32[6,52,2,128]{3,2,1,0:T(2,128)S(1)}, u32[]{:S(2)}, u32[]{:S(2)}) collective-permute-start(f32[6,52,2,128]{3,2,1,0:T(2,128)S(1)} %get-tuple-element.17), channel_id=1, source_target_pairs={{2,0},{4,2},{6,4},{3,1},{5,3},{7,5},{10,8},{12,10},{14,12},{11,9},... | collective-permute-start | bytes 958472 | tf_op jit(solution)/shard_map/ppermute | solution.py:17
  17.9 2.9 %collective-permute-done.2 = f32[6,52,2,128]{3,2,1,0:T(2,128)S(1)} collective-permute-done((f32[6,52,2,128]{3,2,1,0:T(2,128)S(1)}, f32[6,52,2,128]{3,2,1,0:T(2,128)S(1)}, u32[]{:S(2)}, u32[]{:S(2)}) %collective-permute-start.2) | collective-permute-done | bytes 319520 | tf_op jit(solution)/shard_map/ppermute | solution.py:16
  20.8 3.5 %collective-permute-done.3 = f32[6,52,2,128]{3,2,1,0:T(2,128)S(1)} collective-permute-done((f32[6,52,2,128]{3,2,1,0:T(2,128)S(1)}, f32[6,52,2,128]{3,2,1,0:T(2,128)S(1)}, u32[]{:S(2)}, u32[]{:S(2)}) %collective-permute-start.3) | collective-permute-done | bytes 319520 | tf_op jit(solution)/shard_map/ppermute | solution.py:17
  24.3 0.7 copy-done.7
  25.0 0.6 pad_maximum_fusion.1
  25.6 4.2 %fusion.141 = (f32[6,52,20,2]{3,2,1,0:T(8,128)}, f32[6,52,20,2]{3,2,1,0:T(8,128)}) fusion(f32[6,52,20,128]{3,2,1,0:T(8,128)S(1)} %pad_maximum_fusion.1), kind=kLoop, calls=%fused_computation.263 | loop fusion | bytes 199680 | tf_op jit(solution)/shard_map/slice | solution.py:14
  29.8 2.8 %copy.23 = f32[6,52,20,2]{1,3,2,0:T(2,128)S(1)} copy(f32[6,52,20,2]{3,2,1,0:T(8,128)} %get-tuple-element.14) | data formatting | bytes 99840 | tf_op jit(solution)/shard_map/slice | solution.py:14
  32.7 1.3 collective-permute-start.4
  34.0 3.4 %copy.24 = f32[6,52,20,2]{1,3,2,0:T(2,128)} copy(f32[6,52,20,2]{3,2,1,0:T(8,128)} %get-tuple-element.15) | data formatting | bytes 99840 | tf_op jit(solution)/shard_map/slice | solution.py:15
  37.4 5.9 %collective-permute-start.5 = (f32[6,52,20,2]{1,3,2,0:T(2,128)}, f32[6,52,20,2]{1,3,2,0:T(2,128)}, u32[]{:S(2)}, u32[]{:S(2)}) collective-permute-start(f32[6,52,20,2]{1,3,2,0:T(2,128)} %copy.24), channel_id=1, source_target_pairs={{1,0},{3,2},{5,4},{7,6},{9,8},{11,10},{13,12},{15,14},{17,16},{19,... | collective-permute-start | bytes 149768 | tf_op jit(solution)/shard_map/ppermute | solution.py:17
  43.3 3.6 %copy.25 = f32[6,52,20,2]{3,2,1,0:T(8,128)} copy(f32[6,52,20,2]{1,3,2,0:T(2,128)} %collective-permute-done.4) | data formatting | bytes 99840 | tf_op jit(solution)/shard_map/ppermute | solution.py:16
  46.9 3.7 %copy.26 = f32[6,52,20,2]{3,2,1,0:T(8,128)} copy(f32[6,52,20,2]{1,3,2,0:T(2,128)} %collective-permute-done.5) | data formatting | bytes 99840 | tf_op jit(solution)/shard_map/ppermute | solution.py:17
  50.6 8.5 %pad_maximum_fusion = f32[6,52,20,132]{3,2,1,0:T(8,128)S(1)} fusion(f32[6,52,20,2]{3,2,1,0:T(8,128)} %copy.26, f32[6,52,2,128]{3,2,1,0:T(2,128)} %copy-done.7, f32[6,2,16,128]{3,2,1,0:T(8,128)S(1)} %collective-permute-done.1, f32[6,48,16,128]{3,2,1,0:T(8,128)S(1)} %bitcast_dynamic-update-slice_fusion, f32[6,2,16,128]{3,2,1,0:T(8,128)S(1)} %collective-permute-done, ...), kind=kLoop, calls=%fused_computation | loop fusion | flops 4942080 | bytes 6589440 | tf_op jit(solution)/shard_map/concatenate | solution.py:18
  59.1 0.8 slice_bitcast_fusion.2
  59.9 5.1 %and_select_fusion = (f32[50,18,130]{2,1,0:T(8,128)S(1)}, f32[50,18,130]{2,1,0:T(8,128)S(1)}) fusion(f32[52,20,132]{2,1,0:T(8,128)S(1)} %get-tuple-element.11, pred[130]{0:T(512)(128)(4,1)S(1)} %compare_and_fusion, pred[50,18]{1,0:T(8,128)(4,1)S(1)} %broadcast_and_fusion, f32[52,20,132]{2,1,0:T(8,128)S(1)} %get-tuple-element.13, ...), kind=kLoop, calls=%fused_computation.2 | loop fusion | flops 4563000 | bytes 8893030 | tf_op jit(solution)/shard_map/jit(_where)/select_n | solution.py:123
  65.1 5.2 %and_select_fusion.1 = f32[50,18,130]{2,1,0:T(8,128)S(1)} fusion(f32[50,18,130]{2,1,0:T(8,128)S(1)} %get-tuple-element.7, f32[52,20,132]{2,1,0:T(8,128)S(1)} %get-tuple-element.8, f32[52,20,132]{2,1,0:T(8,128)S(1)} %get-tuple-element.12, f32[52,20,132]{2,1,0:T(8,128)S(1)} %get-tuple-element.11, f32[52,20,132]{2,1,0:T(8,128)S(1)} %get-tuple-element.13, ...), kind=kLoop, calls=%fused_computation.3 | loop fusion | flops 4563000 | bytes 8425030 | tf_op jit(solution)/shard_map/jit(_where)/select_n | solution.py:124
  70.3 3.9 %fusion.107 = (f32[48,16,128]{2,1,0:T(8,128)S(1)}, f32[48,16,128]{2,1,0:T(8,128)}) fusion(f32[52,20,132]{2,1,0:T(8,128)S(1)} %get-tuple-element.12, f32[50,18,130]{2,1,0:T(8,128)S(1)} %and_select_fusion.1, f32[48,16,128]{2,1,0:T(8,128)S(1)} %copy-done.3, f32[48,16,128]{2,1,0:T(8,128)S(1)} %copy-done.5, f32[52,20,132]{2,1,0:T(8,128)S(1)} %get-tuple-element.9, ...), kind=kLoop, calls=%fused_computation.185 | loop fusion | flops 8454144 | bytes 13369344 | tf_op jit(solution)/shard_map/sub | solution.py:133
  74.2 5.0 %reshape.66 = f32[6,8,2,8,16,8]{5,4,3,2,1,0:T(8,128)} reshape(f32[48,16,128]{2,1,0:T(8,128)S(1)} %get-tuple-element.4) | data formatting | bytes 786432 | tf_op jit(solution)/shard_map/reshape | solution.py:73
  79.2 3.3 %reduce_sum.19 = f32[6,2,16]{2,1,0:T(2,128)S(1)} reduce(f32[6,8,2,8,16,8]{5,4,3,2,1,0:T(8,128)} %reshape.66, f32[]{:T(128)} %constant.15.clone.1), dimensions={1,3,5}, to_apply=%region_1.2 | reduce | flops 98112 | bytes 393988 | tf_op jit(solution)/shard_map/reduce_sum | solution.py:73
  82.5 3.2 %broadcast_in_dim.36 = f32[6,8,2,8,16,8]{5,4,3,2,1,0:T(8,128)} broadcast(f32[6,2,16]{2,1,0:T(2,128)S(1)} %multiply_multiply_fusion), dimensions={0,2,4} | broadcast | bytes 393984 | tf_op jit(solution)/shard_map/broadcast_in_dim | solution.py:79
  85.7 5.9 %reshape.67 = f32[48,16,128]{2,1,0:T(8,128)} reshape(f32[6,8,2,8,16,8]{5,4,3,2,1,0:T(8,128)} %broadcast_in_dim.36) | data formatting | bytes 786432 | tf_op jit(solution)/shard_map/reshape | solution.py:79
  91.6 1.1 multiply_divide_fusion
  92.7 3.2 %collective-permute-start.6 = (f32[1,16,128]{2,1,0:T(8,128)S(1)}, f32[1,16,128]{2,1,0:T(8,128)S(1)}, u32[]{:S(2)}, u32[]{:S(2)}) collective-permute-start(f32[1,16,128]{2,1,0:T(8,128)S(1)} %get-tuple-element.31), channel_id=1, source_target_pairs={{8,0},{16,8},{24,16},{9,1},{17,9},{25,17},{10,2},{18,10},{26,18},{... | collective-permute-start | bytes 24584 | tf_op jit(solution)/shard_map/ppermute | solution.py:17
  95.9 1.9 %collective-permute-start.7 = (f32[1,16,128]{2,1,0:T(8,128)S(1)}, f32[1,16,128]{2,1,0:T(8,128)S(1)}, u32[]{:S(2)}, u32[]{:S(2)}) collective-permute-start(f32[1,16,128]{2,1,0:T(8,128)S(1)} %get-tuple-element.30), channel_id=1, source_target_pairs={{0,8},{8,16},{16,24},{1,9},{9,17},{17,25},{2,10},{10,18},{18,26},{... | collective-permute-start | bytes 24584 | tf_op jit(solution)/shard_map/ppermute | solution.py:16
  97.8 3.0 %collective-permute-done.7 = f32[1,16,128]{2,1,0:T(8,128)S(1)} collective-permute-done((f32[1,16,128]{2,1,0:T(8,128)S(1)}, f32[1,16,128]{2,1,0:T(8,128)S(1)}, u32[]{:S(2)}, u32[]{:S(2)}) %collective-permute-start.7) | collective-permute-done | bytes 8224 | tf_op jit(solution)/shard_map/ppermute | solution.py:16
  100.9 2.4 %collective-permute-start.8 = (f32[50,1,128]{2,1,0:T(1,128)S(1)}, f32[50,1,128]{2,1,0:T(1,128)S(1)}, u32[]{:S(2)}, u32[]{:S(2)}) collective-permute-start(f32[50,1,128]{2,1,0:T(1,128)S(1)} %get-tuple-element.27), channel_id=1, source_target_pairs={{2,0},{4,2},{6,4},{3,1},{5,3},{7,5},{10,8},{12,10},{14,12},{11,9},... | collective-permute-start | bytes 76808 | tf_op jit(solution)/shard_map/ppermute | solution.py:17
  103.3 3.5 %collective-permute-start.9 = (f32[50,1,128]{2,1,0:T(1,128)S(1)}, f32[50,1,128]{2,1,0:T(1,128)S(1)}, u32[]{:S(2)}, u32[]{:S(2)}) collective-permute-start(f32[50,1,128]{2,1,0:T(1,128)S(1)} %get-tuple-element.26), channel_id=1, source_target_pairs={{0,2},{2,4},{4,6},{1,3},{3,5},{5,7},{8,10},{10,12},{12,14},{9,11},... | collective-permute-start | bytes 76808 | tf_op jit(solution)/shard_map/ppermute | solution.py:16
  106.8 2.2 %collective-permute-done.9 = f32[50,1,128]{2,1,0:T(1,128)S(1)} collective-permute-done((f32[50,1,128]{2,1,0:T(1,128)S(1)}, f32[50,1,128]{2,1,0:T(1,128)S(1)}, u32[]{:S(2)}, u32[]{:S(2)}) %collective-permute-start.9) | collective-permute-done | bytes 25632 | tf_op jit(solution)/shard_map/ppermute | solution.py:16
  109.0 0.1 pad_maximum_fusion.2
  109.1 1.2 fusion.144
  110.3 1.3 copy.27
  111.6 2.6 %collective-permute-start.10 = (f32[50,18,1]{0,2,1:T(1,128)S(1)}, f32[50,18,1]{0,2,1:T(1,128)S(1)}, u32[]{:S(2)}, u32[]{:S(2)}) collective-permute-start(f32[50,18,1]{0,2,1:T(1,128)S(1)} %copy.27), channel_id=1, source_target_pairs={{1,0},{3,2},{5,4},{7,6},{9,8},{11,10},{13,12},{15,14},{17,16},{19,... | collective-permute-start | bytes 10808 | tf_op jit(solution)/shard_map/ppermute | solution.py:17
  114.2 1.3 copy.29
  115.5 1.3 collective-permute-start.11
  116.8 1.2 copy.28
  118.0 3.1 %collective-permute-done.11 = f32[50,18,1]{0,2,1:T(1,128)S(1)} collective-permute-done((f32[50,18,1]{0,2,1:T(1,128)S(1)}, f32[50,18,1]{0,2,1:T(1,128)S(1)}, u32[]{:S(2)}, u32[]{:S(2)}) %collective-permute-start.11) | collective-permute-done | bytes 3632 | tf_op jit(solution)/shard_map/ppermute | solution.py:16
  121.1 1.2 copy.30
  122.2 4.1 %fusion.42 = (f32[48,16,128]{2,1,0:T(8,128)}, f32[48,16,128]{2,1,0:T(8,128)S(1)}) fusion(f32[48,16,128]{2,1,0:T(8,128)} %param.12, f32[50,18,130]{2,1,0:T(8,128)} %copy-done.2, f32[48,16,128]{2,1,0:T(8,128)} %get-tuple-element.5, f32[48,16,128]{2,1,0:T(8,128)} %reshape.67, f32[48,16,128]{2,1,0:T(8,128)} %param.14, ...), kind=kLoop, calls=%fused_computation.77 | loop fusion | flops 5898240 | bytes 5973024 | tf_op jit(solution)/shard_map/sub | solution.py:152
  126.3 1.9 %collective-permute-start.12 = (f32[1,16,128]{2,1,0:T(8,128)S(1)}, f32[1,16,128]{2,1,0:T(8,128)S(1)}, u32[]{:S(2)}, u32[]{:S(2)}) collective-permute-start(f32[1,16,128]{2,1,0:T(8,128)S(1)} %get-tuple-element.29), channel_id=1, source_target_pairs={{8,0},{16,8},{24,16},{9,1},{17,9},{25,17},{10,2},{18,10},{26,18},{... | collective-permute-start | bytes 24584 | tf_op jit(solution)/shard_map/ppermute | solution.py:17
  128.3 2.4 %collective-permute-start.13 = (f32[1,16,128]{2,1,0:T(8,128)S(1)}, f32[1,16,128]{2,1,0:T(8,128)S(1)}, u32[]{:S(2)}, u32[]{:S(2)}) collective-permute-start(f32[1,16,128]{2,1,0:T(8,128)S(1)} %get-tuple-element.28), channel_id=1, source_target_pairs={{0,8},{8,16},{16,24},{1,9},{9,17},{17,25},{2,10},{10,18},{18,26},{... | collective-permute-start | bytes 24584 | tf_op jit(solution)/shard_map/ppermute | solution.py:16
  130.7 2.5 %collective-permute-done.13 = f32[1,16,128]{2,1,0:T(8,128)S(1)} collective-permute-done((f32[1,16,128]{2,1,0:T(8,128)S(1)}, f32[1,16,128]{2,1,0:T(8,128)S(1)}, u32[]{:S(2)}, u32[]{:S(2)}) %collective-permute-start.13) | collective-permute-done | bytes 8224 | tf_op jit(solution)/shard_map/ppermute | solution.py:16
  133.3 2.4 %collective-permute-start.14 = (f32[50,1,128]{2,1,0:T(1,128)S(1)}, f32[50,1,128]{2,1,0:T(1,128)S(1)}, u32[]{:S(2)}, u32[]{:S(2)}) collective-permute-start(f32[50,1,128]{2,1,0:T(1,128)S(1)} %get-tuple-element.25), channel_id=1, source_target_pairs={{2,0},{4,2},{6,4},{3,1},{5,3},{7,5},{10,8},{12,10},{14,12},{11,9},... | collective-permute-start | bytes 76808 | tf_op jit(solution)/shard_map/ppermute | solution.py:17
  135.7 3.5 %collective-permute-start.15 = (f32[50,1,128]{2,1,0:T(1,128)S(1)}, f32[50,1,128]{2,1,0:T(1,128)S(1)}, u32[]{:S(2)}, u32[]{:S(2)}) collective-permute-start(f32[50,1,128]{2,1,0:T(1,128)S(1)} %get-tuple-element.24), channel_id=1, source_target_pairs={{0,2},{2,4},{4,6},{1,3},{3,5},{5,7},{8,10},{10,12},{12,14},{9,11},... | collective-permute-start | bytes 76808 | tf_op jit(solution)/shard_map/ppermute | solution.py:16
  139.1 2.2 %collective-permute-done.15 = f32[50,1,128]{2,1,0:T(1,128)S(1)} collective-permute-done((f32[50,1,128]{2,1,0:T(1,128)S(1)}, f32[50,1,128]{2,1,0:T(1,128)S(1)}, u32[]{:S(2)}, u32[]{:S(2)}) %collective-permute-start.15) | collective-permute-done | bytes 25632 | tf_op jit(solution)/shard_map/ppermute | solution.py:16
  141.4 0.1 pad_maximum_fusion.3
  141.5 1.2 fusion.143
  142.7 1.4 copy.31
  144.1 1.6 %collective-permute-start.16 = (f32[50,18,1]{0,2,1:T(1,128)S(1)}, f32[50,18,1]{0,2,1:T(1,128)S(1)}, u32[]{:S(2)}, u32[]{:S(2)}) collective-permute-start(f32[50,18,1]{0,2,1:T(1,128)S(1)} %copy.31), channel_id=1, source_target_pairs={{1,0},{3,2},{5,4},{7,6},{9,8},{11,10},{13,12},{15,14},{17,16},{19,... | collective-permute-start | bytes 10808 | tf_op jit(solution)/shard_map/ppermute | solution.py:17
  145.8 1.3 copy.33
  147.1 1.3 collective-permute-start.17
  148.4 1.2 copy.32
  149.5 3.1 %collective-permute-done.17 = f32[50,18,1]{0,2,1:T(1,128)S(1)} collective-permute-done((f32[50,18,1]{0,2,1:T(1,128)S(1)}, f32[50,18,1]{0,2,1:T(1,128)S(1)}, u32[]{:S(2)}, u32[]{:S(2)}) %collective-permute-start.17) | collective-permute-done | bytes 3632 | tf_op jit(solution)/shard_map/ppermute | solution.py:16
  152.6 1.2 copy.34
  153.8 5.6 %fusion.45 = f32[48,16,128]{2,1,0:T(8,128)} fusion(f32[52,20,132]{2,1,0:T(8,128)S(1)} %get-tuple-element.11, f32[48,16,128]{2,1,0:T(8,128)S(1)} %get-tuple-element.3, f32[50,18,1]{2,1,0:T(8,128)} %copy.34, f32[50,1,128]{2,1,0:T(1,128)S(1)} %collective-permute-done.14, f32[50,1,128]{2,1,0:T(1,128)S(1)} %collective-permute-done.15, ...), kind=kLoop, calls=%fused_computation.81 | loop fusion | flops 9338880 | bytes 6834240 | tf_op jit(solution)/shard_map/add | solution.py:151
  (44 shorter events, 0.4 us)
Async XLA Ops:
  0.6 2.2 %copy-start.8 = (f32[48,16,128]{2,1,0:T(8,128)S(1)}, f32[48,16,128]{2,1,0:T(8,128)}, u32[]{:S(2)}) copy-start(f32[48,16,128]{2,1,0:T(8,128)} %param.11) | copy-start | bytes 1179652
  0.6 2.3 %copy-start.6 = (f32[48,16,128]{2,1,0:T(8,128)S(1)}, f32[48,16,128]{2,1,0:T(8,128)}, u32[]{:S(2)}) copy-start(f32[48,16,128]{2,1,0:T(8,128)} %param.14) | copy-start | bytes 1179652
  1.7 1.2 copy-start.3
  2.8 1.0 copy-start.4
  2.9 6.6 %copy-start.9 = (s32[6,2,16]{2,1,0:T(2,128)S(1)}, s32[6,2,16]{2,1,0:T(2,128)}, u32[]{:S(2)}) copy-start(s32[6,2,16]{2,1,0:T(2,128)} %param.16) | copy-start | bytes 2308
  2.9 6.6 %copy-start.11 = (f32[4]{0:T(128)S(1)}, f32[4]{0:T(128)}, u32[]{:S(2)}) copy-start(f32[4]{0:T(128)} %param.17) | copy-start | bytes 52
  3.9 5.9 %collective-permute-start = (f32[6,2,16,128]{3,2,1,0:T(8,128)S(1)}, f32[6,2,16,128]{3,2,1,0:T(8,128)S(1)}, u32[]{:S(2)}, u32[]{:S(2)}) collective-permute-start(f32[6,2,16,128]{3,2,1,0:T(8,128)S(1)} %get-tuple-element.18), channel_id=1, source_target_pairs={{0,8},{8,16},{16,24},{1,9},{9,17},{17,25},{2,10},{10,18},{18,26},{... | collective-permute-start | bytes 294920 | tf_op jit(solution)/shard_map/ppermute | solution.py:16
  5.8 5.8 %collective-permute-start.1 = (f32[6,2,16,128]{3,2,1,0:T(8,128)S(1)}, f32[6,2,16,128]{3,2,1,0:T(8,128)S(1)}, u32[]{:S(2)}, u32[]{:S(2)}) collective-permute-start(f32[6,2,16,128]{3,2,1,0:T(8,128)S(1)} %get-tuple-element.19), channel_id=1, source_target_pairs={{8,0},{16,8},{24,16},{9,1},{17,9},{25,17},{10,2},{18,10},{26,18},{... | collective-permute-start | bytes 294920 | tf_op jit(solution)/shard_map/ppermute | solution.py:17
  11.9 8.9 %collective-permute-start.2 = (f32[6,52,2,128]{3,2,1,0:T(2,128)S(1)}, f32[6,52,2,128]{3,2,1,0:T(2,128)S(1)}, u32[]{:S(2)}, u32[]{:S(2)}) collective-permute-start(f32[6,52,2,128]{3,2,1,0:T(2,128)S(1)} %get-tuple-element.16), channel_id=1, source_target_pairs={{0,2},{2,4},{4,6},{1,3},{3,5},{5,7},{8,10},{10,12},{12,14},{9,11},... | collective-permute-start | bytes 958472 | tf_op jit(solution)/shard_map/ppermute | solution.py:16
  15.4 8.9 %collective-permute-start.3 = (f32[6,52,2,128]{3,2,1,0:T(2,128)S(1)}, f32[6,52,2,128]{3,2,1,0:T(2,128)S(1)}, u32[]{:S(2)}, u32[]{:S(2)}) collective-permute-start(f32[6,52,2,128]{3,2,1,0:T(2,128)S(1)} %get-tuple-element.17), channel_id=1, source_target_pairs={{2,0},{4,2},{6,4},{3,1},{5,3},{7,5},{10,8},{12,10},{14,12},{11,9},... | collective-permute-start | bytes 958472 | tf_op jit(solution)/shard_map/ppermute | solution.py:17
  24.3 0.7 copy-start.7
  32.7 10.6 %collective-permute-start.4 = (f32[6,52,20,2]{1,3,2,0:T(2,128)S(1)}, f32[6,52,20,2]{1,3,2,0:T(2,128)}, u32[]{:S(2)}, u32[]{:S(2)}) collective-permute-start(f32[6,52,20,2]{1,3,2,0:T(2,128)S(1)} %copy.23), channel_id=1, source_target_pairs={{0,1},{2,3},{4,5},{6,7},{8,9},{10,11},{12,13},{14,15},{16,17},{18,... | collective-permute-start | bytes 149768 | tf_op jit(solution)/shard_map/ppermute | solution.py:16
  37.4 9.5 %collective-permute-start.5 = (f32[6,52,20,2]{1,3,2,0:T(2,128)}, f32[6,52,20,2]{1,3,2,0:T(2,128)}, u32[]{:S(2)}, u32[]{:S(2)}) collective-permute-start(f32[6,52,20,2]{1,3,2,0:T(2,128)} %copy.24), channel_id=1, source_target_pairs={{1,0},{3,2},{5,4},{7,6},{9,8},{11,10},{13,12},{15,14},{17,16},{19,... | collective-permute-start | bytes 149768 | tf_op jit(solution)/shard_map/ppermute | solution.py:17
  65.0 5.2 %copy-start.2 = (f32[50,18,130]{2,1,0:T(8,128)}, f32[50,18,130]{2,1,0:T(8,128)S(1)}, u32[]{:S(2)}) copy-start(f32[50,18,130]{2,1,0:T(8,128)S(1)} %get-tuple-element.7) | copy-start | bytes 1404004
  65.0 5.2 %copy-start = (f32[50,18,130]{2,1,0:T(8,128)}, f32[50,18,130]{2,1,0:T(8,128)S(1)}, u32[]{:S(2)}) copy-start(f32[50,18,130]{2,1,0:T(8,128)S(1)} %get-tuple-element.6) | copy-start | bytes 1404004
  65.1 5.2 %copy-start.5 = (f32[48,16,128]{2,1,0:T(8,128)S(1)}, f32[48,16,128]{2,1,0:T(8,128)}, u32[]{:S(2)}) copy-start(f32[48,16,128]{2,1,0:T(8,128)} %param.13) | copy-start | bytes 1179652
  79.2 3.3 %copy-start.10 = (s32[6,2,16]{2,1,0:T(2,128)S(1)}, s32[6,2,16]{2,1,0:T(2,128)}, u32[]{:S(2)}) copy-start(s32[6,2,16]{2,1,0:T(2,128)} %param.15) | copy-start | bytes 2308
  92.7 5.1 %collective-permute-start.6 = (f32[1,16,128]{2,1,0:T(8,128)S(1)}, f32[1,16,128]{2,1,0:T(8,128)S(1)}, u32[]{:S(2)}, u32[]{:S(2)}) collective-permute-start(f32[1,16,128]{2,1,0:T(8,128)S(1)} %get-tuple-element.31), channel_id=1, source_target_pairs={{8,0},{16,8},{24,16},{9,1},{17,9},{25,17},{10,2},{18,10},{26,18},{... | collective-permute-start | bytes 24584 | tf_op jit(solution)/shard_map/ppermute | solution.py:17
  95.9 5.0 %collective-permute-start.7 = (f32[1,16,128]{2,1,0:T(8,128)S(1)}, f32[1,16,128]{2,1,0:T(8,128)S(1)}, u32[]{:S(2)}, u32[]{:S(2)}) collective-permute-start(f32[1,16,128]{2,1,0:T(8,128)S(1)} %get-tuple-element.30), channel_id=1, source_target_pairs={{0,8},{8,16},{16,24},{1,9},{9,17},{17,25},{2,10},{10,18},{18,26},{... | collective-permute-start | bytes 24584 | tf_op jit(solution)/shard_map/ppermute | solution.py:16
  100.9 5.9 %collective-permute-start.8 = (f32[50,1,128]{2,1,0:T(1,128)S(1)}, f32[50,1,128]{2,1,0:T(1,128)S(1)}, u32[]{:S(2)}, u32[]{:S(2)}) collective-permute-start(f32[50,1,128]{2,1,0:T(1,128)S(1)} %get-tuple-element.27), channel_id=1, source_target_pairs={{2,0},{4,2},{6,4},{3,1},{5,3},{7,5},{10,8},{12,10},{14,12},{11,9},... | collective-permute-start | bytes 76808 | tf_op jit(solution)/shard_map/ppermute | solution.py:17
  103.3 5.7 %collective-permute-start.9 = (f32[50,1,128]{2,1,0:T(1,128)S(1)}, f32[50,1,128]{2,1,0:T(1,128)S(1)}, u32[]{:S(2)}, u32[]{:S(2)}) collective-permute-start(f32[50,1,128]{2,1,0:T(1,128)S(1)} %get-tuple-element.26), channel_id=1, source_target_pairs={{0,2},{2,4},{4,6},{1,3},{3,5},{5,7},{8,10},{10,12},{12,14},{9,11},... | collective-permute-start | bytes 76808 | tf_op jit(solution)/shard_map/ppermute | solution.py:16
  111.6 5.2 %collective-permute-start.10 = (f32[50,18,1]{0,2,1:T(1,128)S(1)}, f32[50,18,1]{0,2,1:T(1,128)S(1)}, u32[]{:S(2)}, u32[]{:S(2)}) collective-permute-start(f32[50,18,1]{0,2,1:T(1,128)S(1)} %copy.27), channel_id=1, source_target_pairs={{1,0},{3,2},{5,4},{7,6},{9,8},{11,10},{13,12},{15,14},{17,16},{19,... | collective-permute-start | bytes 10808 | tf_op jit(solution)/shard_map/ppermute | solution.py:17
  115.5 5.6 %collective-permute-start.11 = (f32[50,18,1]{0,2,1:T(1,128)S(1)}, f32[50,18,1]{0,2,1:T(1,128)S(1)}, u32[]{:S(2)}, u32[]{:S(2)}) collective-permute-start(f32[50,18,1]{0,2,1:T(1,128)S(1)} %copy.29), channel_id=1, source_target_pairs={{0,1},{2,3},{4,5},{6,7},{8,9},{10,11},{12,13},{14,15},{16,17},{18,... | collective-permute-start | bytes 10808 | tf_op jit(solution)/shard_map/ppermute | solution.py:16
  126.3 4.3 %collective-permute-start.12 = (f32[1,16,128]{2,1,0:T(8,128)S(1)}, f32[1,16,128]{2,1,0:T(8,128)S(1)}, u32[]{:S(2)}, u32[]{:S(2)}) collective-permute-start(f32[1,16,128]{2,1,0:T(8,128)S(1)} %get-tuple-element.29), channel_id=1, source_target_pairs={{8,0},{16,8},{24,16},{9,1},{17,9},{25,17},{10,2},{18,10},{26,18},{... | collective-permute-start | bytes 24584 | tf_op jit(solution)/shard_map/ppermute | solution.py:17
  128.3 5.0 %collective-permute-start.13 = (f32[1,16,128]{2,1,0:T(8,128)S(1)}, f32[1,16,128]{2,1,0:T(8,128)S(1)}, u32[]{:S(2)}, u32[]{:S(2)}) collective-permute-start(f32[1,16,128]{2,1,0:T(8,128)S(1)} %get-tuple-element.28), channel_id=1, source_target_pairs={{0,8},{8,16},{16,24},{1,9},{9,17},{17,25},{2,10},{10,18},{18,26},{... | collective-permute-start | bytes 24584 | tf_op jit(solution)/shard_map/ppermute | solution.py:16
  133.3 5.9 %collective-permute-start.14 = (f32[50,1,128]{2,1,0:T(1,128)S(1)}, f32[50,1,128]{2,1,0:T(1,128)S(1)}, u32[]{:S(2)}, u32[]{:S(2)}) collective-permute-start(f32[50,1,128]{2,1,0:T(1,128)S(1)} %get-tuple-element.25), channel_id=1, source_target_pairs={{2,0},{4,2},{6,4},{3,1},{5,3},{7,5},{10,8},{12,10},{14,12},{11,9},... | collective-permute-start | bytes 76808 | tf_op jit(solution)/shard_map/ppermute | solution.py:17
  135.7 5.7 %collective-permute-start.15 = (f32[50,1,128]{2,1,0:T(1,128)S(1)}, f32[50,1,128]{2,1,0:T(1,128)S(1)}, u32[]{:S(2)}, u32[]{:S(2)}) collective-permute-start(f32[50,1,128]{2,1,0:T(1,128)S(1)} %get-tuple-element.24), channel_id=1, source_target_pairs={{0,2},{2,4},{4,6},{1,3},{3,5},{5,7},{8,10},{10,12},{12,14},{9,11},... | collective-permute-start | bytes 76808 | tf_op jit(solution)/shard_map/ppermute | solution.py:16
  142.7 11.1 %copy-start.1 = (f32[50,18,130]{2,1,0:T(8,128)S(1)}, f32[50,18,130]{2,1,0:T(8,128)}, u32[]{:S(2)}) copy-start(f32[50,18,130]{2,1,0:T(8,128)} %copy-done) | copy-start | bytes 1404004
  144.1 4.3 %collective-permute-start.16 = (f32[50,18,1]{0,2,1:T(1,128)S(1)}, f32[50,18,1]{0,2,1:T(1,128)S(1)}, u32[]{:S(2)}, u32[]{:S(2)}) collective-permute-start(f32[50,18,1]{0,2,1:T(1,128)S(1)} %copy.31), channel_id=1, source_target_pairs={{1,0},{3,2},{5,4},{7,6},{9,8},{11,10},{13,12},{15,14},{17,16},{19,... | collective-permute-start | bytes 10808 | tf_op jit(solution)/shard_map/ppermute | solution.py:17
  147.1 5.6 %collective-permute-start.17 = (f32[50,18,1]{0,2,1:T(1,128)S(1)}, f32[50,18,1]{0,2,1:T(1,128)S(1)}, u32[]{:S(2)}, u32[]{:S(2)}) collective-permute-start(f32[50,18,1]{0,2,1:T(1,128)S(1)} %copy.33), channel_id=1, source_target_pairs={{0,1},{2,3},{4,5},{6,7},{8,9},{10,11},{12,13},{14,15},{16,17},{18,... | collective-permute-start | bytes 10808 | tf_op jit(solution)/shard_map/ppermute | solution.py:16
where the time goes:
time: 160 us; the launch traced here: 159 us
  local copies, waits for them, and re-layouts  49.1 us (31%)
  starting transfers between devices  46.4 us (29%)
  other arithmetic  38 us (24%)
  waiting for transfers between devices  24.7 us (15%)
    ppermute x9, starting transfers between devices, extended(): after = lax.ppermute(leading, axis, down)  25.9 us
    ppermute x9, starting transfers between devices, extended(): before = lax.ppermute(last, axis, up)  20.5 us
    ppermute x9, waiting for transfers between devices, extended(): before = lax.ppermute(last, axis, up)  19.3 us
    slice x7, local copies, waits for them, and re-layouts, extended(): last = lax.slice_in_dim(x, length - width, length, axis=dim)  9.7 us
    concatenate x6, other arithmetic, extended(): x = jnp.concatenate([before, x, after], axis=dim)  9.34 us
    slice x5, local copies, waits for them, and re-layouts, extended(): leading = lax.slice_in_dim(x, 0, width, axis=dim)  8.57 us
    ppermute x3, local copies, waits for them, and re-layouts, extended(): after = lax.ppermute(leading, axis, down)  6.01 us
    ppermute x3, local copies, waits for them, and re-layouts, extended(): before = lax.ppermute(last, axis, up)  5.97 us
  transfers between devices with their start and end apart: 18, of which 10 were waited for; matrix products, arithmetic and copies ran while one was open for 8% of the time, Pallas kernels for 0%

commit v1 on v0

v1 whole, which is shorter than its diff:
```python
import functools

import jax
import jax.numpy as jnp
from jax import lax
from jax.experimental import pallas as pl
from jax.experimental.pallas import tpu as pltpu
from jax.sharding import PartitionSpec as P

time_step = 0.1
MESH = pl.DeviceIdType.MESH
AXES = ("gx", "gy", "gz")
TOP = 8
EDGE = 8
VOXEL = 8
EXACT = lax.Precision.HIGHEST


def kernel(
    conc, disp, step, vel, cap_in, capstep_in, mask, label, class_weight,
    out_d, out_c,
    f_in, f_mid, f_sc, f_first,
    cap, capstep, ratio, rate1, rate2, part, res_d, res_c,
    ys_in, ys_mid, ys_sc, ys_first,
    yr_in, yr_mid, yr_sc, yr_first,
    zs_in, zs_mid, zs_sc, zs_first,
    zr_in, zr_mid, zr_sc, zr_first,
    coarse, weight, load_sem, out_sem, send_sem, recv_sem,
):
    nx, ny, nz = cap.shape
    rows = ny + 2 * EDGE
    place = [lax.axis_index(a) for a in AXES]
    count = [lax.axis_size(a) for a in AXES]
    has_lo = [p > 0 for p in place]
    has_hi = [p < n - 1 for p, n in zip(place, count)]

    def main(ref):
        return ref.at[pl.ds(1, nx), pl.ds(TOP, ny)]

    loads = []
    for i, (src, dst) in enumerate((
        (conc, main(f_in.at[0])), (disp, main(f_in.at[1])), (step, main(f_in.at[2])),
        (vel, main(f_in.at[3])), (cap_in, cap), (capstep_in, capstep),
    )):
        load = pltpu.make_async_copy(src, dst, load_sem.at[i])
        load.start()
        loads.append(load)

    for ref in (f_in, f_mid, f_sc, f_first):
        for k in range(ref.shape[0]):
            for x in (0, nx + 1):
                ref[k, x, TOP:TOP + ny, :] = jnp.zeros((ny, nz), jnp.float32)
    for ref in (yr_in, yr_mid, yr_sc, yr_first, zr_in, zr_mid, zr_sc, zr_first):
        ref[...] = jnp.zeros(ref.shape, jnp.float32)

    barrier = pltpu.get_barrier_semaphore()
    for a, name in enumerate(AXES):
        @pl.when(has_lo[a])
        def _():
            pl.semaphore_signal(barrier, inc=1, device_id={name: place[a] - 1}, device_id_type=MESH)

        @pl.when(has_hi[a])
        def _():
            pl.semaphore_signal(barrier, inc=1, device_id={name: place[a] + 1}, device_id_type=MESH)

    lane = lax.broadcasted_iota(jnp.int32, (ny, nz), 1)
    first_lane = lane == 0
    last_lane = lane == nz - 1
    pair = lane // 2

    def copies(phase, fields, ys, yr, zs, zr):
        k = yr.shape[1]

        def remote(src, dst, axis, side):
            at = (phase * 3 + axis) * 2 + side
            to = place[axis] - 1 if side == 0 else place[axis] + 1
            return pltpu.make_async_remote_copy(
                src_ref=src, dst_ref=dst, send_sem=send_sem.at[at], recv_sem=recv_sem.at[at],
                device_id={AXES[axis]: to}, device_id_type=MESH)

        def slab(x):
            return fields.at[pl.ds(0, k), x, pl.ds(TOP, ny)]

        return [
            (remote(slab(1), slab(nx + 1), 0, 0), remote(slab(nx), slab(0), 0, 1)),
            (remote(ys.at[0], yr.at[1], 1, 0), remote(ys.at[1], yr.at[0], 1, 1)),
            (remote(zs, zr.at[1], 2, 0), remote(zs, zr.at[0], 2, 1)),
        ]

    def start(pairs, axis):
        lo, hi = pairs[axis]

        @pl.when(has_lo[axis])
        def _():
            lo.start()

        @pl.when(has_hi[axis])
        def _():
            hi.start()

    def finish(pairs):
        for axis in range(3):
            lo, hi = pairs[axis]

            @pl.when(has_lo[axis])
            def _():
                hi.wait_recv()
                lo.wait_send()

            @pl.when(has_hi[axis])
            def _():
                lo.wait_recv()
                hi.wait_send()

    def pack_rows(fields, ys, k):
        flat = fields.reshape(fields.shape[0], (nx + 2) * rows, nz)
        for i in range(k):
            ys[0, i] = flat[i, pl.ds(rows + TOP, nx, stride=rows), :]
            ys[1, i] = flat[i, pl.ds(rows + TOP + ny - 1, nx, stride=rows), :]

    def unpack(fields, yr, zr, k):
        flat = fields.reshape(fields.shape[0], (nx + 2) * rows, nz)
        for i in range(k):
            flat[i, pl.ds(rows + TOP - 1, nx, stride=rows), :] = yr[0, i]
            flat[i, pl.ds(rows + TOP + ny, nx, stride=rows), :] = yr[1, i]
        for i in range(zr.shape[1]):
            above = pltpu.roll(zr[1, i], nz - 1, 1)
            below = pltpu.roll(zr[0, i], 1, 1)
            zr[0, i] = jnp.where(lane % 2 == 0, above, below)

    def pack_column(plane, slab, x):
        return jnp.where(pair == x, pltpu.roll(slab, 2 * x + 1, 1), plane)

    def center(fields, i, x):
        return fields[i, x + 1, TOP:TOP + ny, :]

    def ends(zr, i, x):
        return pltpu.roll(zr[0, i], nz - 1 - 2 * x, 1)

    def z_up(v, end):
        return jnp.where(last_lane, end, pltpu.roll(v, nz - 1, 1))

    def z_down(v, end):
        return jnp.where(first_lane, end, pltpu.roll(v, 1, 1))

    def around(fields, i, x, v, zr):
        end = ends(zr, i, x)
        return [
            z_up(v, end), z_down(v, end),
            fields[i, x + 2, TOP:TOP + ny, :], fields[i, x, TOP:TOP + ny, :],
            fields[i, x + 1, TOP + 1:TOP + 1 + ny, :], fields[i, x + 1, TOP - 1:TOP - 1 + ny, :],
        ]

    def total(terms):
        return functools.reduce(lambda p, q: p + q, terms)

    pairs = copies(0, f_in, ys_in, yr_in, zs_in, zr_in)
    for load in loads[:4]:
        load.wait()
    pack_rows(f_in, ys_in, 3)

    pl.semaphore_wait(barrier, sum(h.astype(jnp.int32) for h in has_lo + has_hi))

    start(pairs, 1)
    start(pairs, 0)

    blank = jnp.zeros((ny, nz), jnp.float32)

    def pack_in(x, planes):
        return tuple(pack_column(p, center(f_in, i, x), x) for i, p in enumerate(planes))

    planes = lax.fori_loop(0, nx, pack_in, (blank,) * 4, unroll=4)
    for i in range(4):
        zs_in[i] = planes[i]
    start(pairs, 2)

    sx, sy, sz = mask.shape
    weight[...] = jnp.zeros(weight.shape, jnp.float32)
    for i in range(sx):
        picked = jnp.zeros((sy, sz), jnp.float32)
        for c in range(class_weight.shape[0]):
            picked = picked + jnp.where(label[i] == c, class_weight[c], 0.0)
        weight[i * sy:(i + 1) * sy, 0:sz] = mask[i].astype(jnp.float32) * picked
    spread = (
        lax.broadcasted_iota(jnp.int32, (nz, nz), 0) == lax.broadcasted_iota(jnp.int32, (nz, nz), 1) // VOXEL
    ).astype(jnp.float32)
    weight[...] = jnp.dot(weight[...], spread, precision=EXACT, preferred_element_type=jnp.float32)
    for load in loads[4:]:
        load.wait()

    finish(pairs)
    unpack(f_in, yr_in, zr_in, 3)

    def first(x, planes):
        c, d, s, v = (center(f_in, i, x) for i in range(4))
        cn = around(f_in, 0, x, c, zr_in)
        dn = around(f_in, 1, x, d, zr_in)
        sn = around(f_in, 2, x, s, zr_in)
        v_down = z_down(v, ends(zr_in, 3, x))
        diff = [n - c for n in cn]
        g_d = total([(d + k) * q for k, q in zip(dn, diff)])
        g_s = total([(s + k) * q for k, q in zip(sn, diff)])
        rate = 0.5 * g_d + v_down * cn[1] - v * c
        inv = 1.0 / cap[x]
        r = time_step * inv
        cs = r * inv * capstep[x]
        later = c + r * rate
        tangent = 0.5 * r * g_s - cs * rate
        ratio[x] = r
        capstep[x] = cs
        rate1[x] = rate
        f_mid[0, x + 1, TOP:TOP + ny, :] = later
        f_mid[1, x + 1, TOP:TOP + ny, :] = tangent
        return pack_column(planes[0], later, x), pack_column(planes[1], tangent, x)

    planes = lax.fori_loop(0, nx, first, (blank,) * 2, unroll=2)
    pairs = copies(1, f_mid, ys_mid, yr_mid, zs_mid, zr_mid)
    pack_rows(f_mid, ys_mid, 2)
    start(pairs, 1)
    start(pairs, 0)
    zs_mid[0] = planes[0]
    zs_mid[1] = planes[1]
    start(pairs, 2)
    finish(pairs)
    unpack(f_mid, yr_mid, zr_mid, 2)

    def second_at(x):
        l, t = (center(f_mid, i, x) for i in range(2))
        d, s, v = (center(f_in, i, x) for i in range(1, 4))
        ln = around(f_mid, 0, x, l, zr_mid)
        tn = around(f_mid, 1, x, t, zr_mid)
        dn = around(f_in, 1, x, d, zr_in)
        sn = around(f_in, 2, x, s, zr_in)
        v_down = z_down(v, ends(zr_in, 3, x))
        l_diff = [n - l for n in ln]
        kd = [d + k for k in dn]
        rate = 0.5 * total([k * q for k, q in zip(kd, l_diff)]) + v_down * ln[1] - v * l
        mixed = total([k * (n - t) + (s + m) * q for k, n, m, q in zip(kd, tn, sn, l_diff)])
        rate2[x] = rate
        return t + ratio[x] * (0.5 * mixed + v_down * tn[1] - v * t) - capstep[x] * rate

    def voxel_row(g, carry):
        def one(i, acc):
            return acc + second_at(g * VOXEL + i)

        acc = lax.fori_loop(0, VOXEL, one, blank, unroll=2)
        sums = jnp.concatenate(
            [jnp.sum(acc[j * VOXEL:(j + 1) * VOXEL], axis=0, keepdims=True) for j in range(sy)], axis=0)
        coarse[pl.ds(g * sy, sy), :] = sums
        return carry

    lax.fori_loop(0, sx, voxel_row, 0)
    sums = coarse[...]
    wide = lax.broadcasted_iota(jnp.int32, sums.shape, 1)
    for hop in (1, 2, 4):
        sums = sums + jnp.where((wide & hop) == 0, pltpu.roll(sums, nz - hop, 1), pltpu.roll(sums, hop, 1))
    coarse[...] = weight[...] * (sums * (1.0 / VOXEL**3))

    def source_at(x):
        g = x // VOXEL
        return jnp.concatenate(
            [jnp.broadcast_to(coarse[pl.ds(g * sy + j, 1), :], (VOXEL, nz)) for j in range(sy)], axis=0)

    def scale(x, plane):
        scaled = ratio[x] * source_at(x)
        f_sc[0, x + 1, TOP:TOP + ny, :] = scaled
        return pack_column(plane, scaled, x)

    plane = lax.fori_loop(0, nx, scale, blank, unroll=4)
    pairs = copies(2, f_sc, ys_sc, yr_sc, zs_sc, zr_sc)
    pack_rows(f_sc, ys_sc, 1)
    start(pairs, 1)
    start(pairs, 0)
    zs_sc[0] = plane
    start(pairs, 2)
    finish(pairs)
    unpack(f_sc, yr_sc, zr_sc, 1)

    def third(x, plane):
        d, v = center(f_in, 1, x), center(f_in, 3, x)
        w = center(f_sc, 0, x)
        dn = around(f_in, 1, x, d, zr_in)
        wn = around(f_sc, 0, x, w, zr_sc)
        g = total([(d + k) * (n - w) for k, n in zip(dn, wn)])
        earlier = source_at(x) + 0.5 * g + v * (wn[0] - w)
        r = ratio[x]
        one = r * earlier
        f_first[0, x + 1, TOP:TOP + ny, :] = one
        return pack_column(plane, one, x)

    plane = lax.fori_loop(0, nx, third, blank, unroll=2)
    pairs = copies(3, f_first, ys_first, yr_first, zs_first, zr_first)
    pack_rows(f_first, ys_first, 1)
    start(pairs, 1)
    start(pairs, 0)
    zs_first[0] = plane
    start(pairs, 2)

    def fourth(x, carry):
        w = center(f_sc, 0, x)
        l = center(f_mid, 0, x)
        one = center(f_first, 0, x)
        wn = around(f_sc, 0, x, w, zr_sc)
        ln = around(f_mid, 0, x, l, zr_mid)
        part[x] = total([(w - m) * (n - l) for m, n in zip(wn, ln)])
        res_c[x] = -(w * rate2[x] + one * rate1[x]) * (ratio[x] * (1.0 / time_step))
        return carry

    lax.fori_loop(0, nx, fourth, 0, unroll=2)
    store_c = pltpu.make_async_copy(res_c, out_c, out_sem.at[0])
    store_c.start()
    finish(pairs)
    unpack(f_first, yr_first, zr_first, 1)

    def fifth(x, carry):
        one = center(f_first, 0, x)
        c = center(f_in, 0, x)
        on = around(f_first, 0, x, one, zr_first)
        cn = around(f_in, 0, x, c, zr_in)
        res_d[x] = 0.5 * (part[x] + total([(one - m) * (n - c) for m, n in zip(on, cn)]))
        return carry

    lax.fori_loop(0, nx, fifth, 0, unroll=2)
    store_d = pltpu.make_async_copy(res_d, out_d, out_sem.at[1])
    store_d.start()
    store_c.wait()
    store_d.wait()


def shards(concentration, dispersion, disp_step, capacity, cap_step, velocity, voxel_mask, voxel_class, class_weight):
    nx, ny, nz = concentration.shape
    f32 = jnp.float32
    block = jax.ShapeDtypeStruct((nx, ny, nz), f32)
    hbm = pl.BlockSpec(memory_space=pl.ANY)
    vmem = pl.BlockSpec(memory_space=pltpu.VMEM)
    smem = pl.BlockSpec(memory_space=pltpu.SMEM)
    whole = pltpu.VMEM((nx, ny, nz), f32)
    coarse_rows = -(-(nx // VOXEL) * (ny // VOXEL) // 8) * 8
    per_phase = (3, 2, 1, 1)
    z_phase = (4, 2, 1, 1)
    fields = (4, 2, 1, 1)
    scratch = (
        [pltpu.VMEM((k, nx + 2, ny + 2 * EDGE, nz), f32) for k in fields]
        + [whole] * 8
        + [pltpu.VMEM((2, k, nx, nz), f32) for k in per_phase]
        + [pltpu.VMEM((2, k, nx, nz), f32) for k in per_phase]
        + [pltpu.VMEM((k, ny, nz), f32) for k in z_phase]
        + [pltpu.VMEM((2, k, ny, nz), f32) for k in z_phase]
        + [pltpu.VMEM((coarse_rows, nz), f32)] * 2
        + [pltpu.SemaphoreType.DMA((6,)), pltpu.SemaphoreType.DMA((2,))]
        + [pltpu.SemaphoreType.DMA((24,))] * 2
    )
    return pl.pallas_call(
        kernel,
        out_shape=(block, block),
        in_specs=[hbm] * 6 + [vmem, vmem, smem],
        out_specs=(hbm, hbm),
        scratch_shapes=scratch,
        compiler_params=pltpu.CompilerParams(
            collective_id=0, has_side_effects=True, vmem_limit_bytes=32 * 1024 * 1024),
    )(concentration, dispersion, disp_step, velocity, capacity, cap_step, voxel_mask, voxel_class, class_weight)


def solution(mesh):
    cube = P("gx", "gy", "gz")
    return jax.shard_map(
        shards, mesh=mesh, in_specs=(cube,) * 8 + (P(),), out_specs=(cube, cube), check_vma=False)
```

time: 160 us -> 46.3 us (0.29)
  the two profiles are of different devices: /device:TPU:22 before, /device:TPU:0 now
where the time goes in v1:
time: 46.3 us; the launch traced here: 45.8 us
  Pallas kernels  35.7 us (77%)
  local copies, waits for them, and re-layouts  9.5 us (21%)
  between operations  0.66 us (1%)
    pallas_call x1, Pallas kernels, shards(): pl.pallas_call(kernel, out_shape=(block, block), in_specs=[hbm] * 6 + [vm...  35.7 us
    unnamed x20, local copies, waits for them, and re-layouts  9.5 us

profile of v1, /device:TPU:0, one launch (start us, length us, event | category | flops | bytes accessed | tf_op | source)
XLA Modules:
  0.0 45.8 jit_solution(3669602039891111293)
XLA Ops:
  0.6 0.0 copy-start
  0.6 1.0 %copy-done = f32[48,16,128]{2,1,0:T(8,128)S(1)} copy-done((f32[48,16,128]{2,1,0:T(8,128)S(1)}, f32[48,16,128]{2,1,0:T(8,128)}, u32[]{:S(2)}) %copy-start) | copy-done | bytes 393240
  1.6 0.0 copy-start.1
  1.6 1.0 %copy-done.1 = f32[48,16,128]{2,1,0:T(8,128)S(1)} copy-done((f32[48,16,128]{2,1,0:T(8,128)S(1)}, f32[48,16,128]{2,1,0:T(8,128)}, u32[]{:S(2)}) %copy-start.1) | copy-done | bytes 393240
  2.6 0.0 copy-start.2
  2.6 1.0 %copy-done.2 = f32[48,16,128]{2,1,0:T(8,128)S(1)} copy-done((f32[48,16,128]{2,1,0:T(8,128)S(1)}, f32[48,16,128]{2,1,0:T(8,128)}, u32[]{:S(2)}) %copy-start.2) | copy-done | bytes 393240
  3.6 0.0 copy-start.3
  3.6 1.0 %copy-done.3 = f32[48,16,128]{2,1,0:T(8,128)S(1)} copy-done((f32[48,16,128]{2,1,0:T(8,128)S(1)}, f32[48,16,128]{2,1,0:T(8,128)}, u32[]{:S(2)}) %copy-start.3) | copy-done | bytes 393240
  4.6 0.0 copy-start.4
  4.6 1.0 %copy-done.4 = f32[48,16,128]{2,1,0:T(8,128)S(1)} copy-done((f32[48,16,128]{2,1,0:T(8,128)S(1)}, f32[48,16,128]{2,1,0:T(8,128)}, u32[]{:S(2)}) %copy-start.4) | copy-done | bytes 393240
  5.6 0.0 copy-start.5
  5.6 1.0 %copy-done.5 = f32[48,16,128]{2,1,0:T(8,128)S(1)} copy-done((f32[48,16,128]{2,1,0:T(8,128)S(1)}, f32[48,16,128]{2,1,0:T(8,128)}, u32[]{:S(2)}) %copy-start.5) | copy-done | bytes 393240
  6.6 0.0 copy-start.6
  6.6 0.7 %copy-done.6 = s32[6,2,16]{2,1,0:T(2,128)S(1)} copy-done((s32[6,2,16]{2,1,0:T(2,128)S(1)}, s32[6,2,16]{2,1,0:T(2,128)}, u32[]{:S(2)}) %copy-start.6) | copy-done | bytes 792
  7.3 0.0 copy-start.7
  7.3 0.7 %copy-done.7 = s32[6,2,16]{2,1,0:T(2,128)S(1)} copy-done((s32[6,2,16]{2,1,0:T(2,128)S(1)}, s32[6,2,16]{2,1,0:T(2,128)}, u32[]{:S(2)}) %copy-start.7) | copy-done | bytes 792
  8.0 0.0 copy-start.8
  8.0 0.7 %copy-done.8 = f32[4]{0:T(128)S(1)} copy-done((f32[4]{0:T(128)S(1)}, f32[4]{0:T(128)}, u32[]{:S(2)}) %copy-start.8) | copy-done | bytes 40
  8.7 35.7 %shard_map.104 = (f32[48,16,128]{2,1,0:T(8,128)S(1)}, f32[48,16,128]{2,1,0:T(8,128)S(1)}) custom-call(f32[48,16,128]{2,1,0:T(8,128)S(1)} %copy-done, f32[48,16,128]{2,1,0:T(8,128)S(1)} %copy-done.1, f32[48,16,128]{2,1,0:T(8,128)S(1)} %copy-done.2, f32[48,16,128]{2,1,0:T(8,128)S(1)} %copy-done.3, f32[48,16,128]{2,1,0:T(8,128)S(1)} %copy-done.4, ...), custom_call_target="tpu_custom_call" | custom-call | tf_op jit(solution)/shard_map/pallas_call | solution.py:353
  44.3 0.7 %copy.13 = f32[48,16,128]{2,1,0:T(8,128)} copy(f32[48,16,128]{2,1,0:T(8,128)S(1)} %get-tuple-element.4) | data formatting | bytes 786432
  45.1 0.7 %copy.14 = f32[48,16,128]{2,1,0:T(8,128)} copy(f32[48,16,128]{2,1,0:T(8,128)S(1)} %get-tuple-element.5) | data formatting | bytes 786432
Async XLA Ops:
  0.6 1.0 %copy-start = (f32[48,16,128]{2,1,0:T(8,128)S(1)}, f32[48,16,128]{2,1,0:T(8,128)}, u32[]{:S(2)}) copy-start(f32[48,16,128]{2,1,0:T(8,128)} %conc.1) | copy-start | bytes 1179652
  1.6 1.0 %copy-start.1 = (f32[48,16,128]{2,1,0:T(8,128)S(1)}, f32[48,16,128]{2,1,0:T(8,128)}, u32[]{:S(2)}) copy-start(f32[48,16,128]{2,1,0:T(8,128)} %disp.1) | copy-start | bytes 1179652
  2.6 1.0 %copy-start.2 = (f32[48,16,128]{2,1,0:T(8,128)S(1)}, f32[48,16,128]{2,1,0:T(8,128)}, u32[]{:S(2)}) copy-start(f32[48,16,128]{2,1,0:T(8,128)} %step.1) | copy-start | bytes 1179652
  3.6 1.0 %copy-start.3 = (f32[48,16,128]{2,1,0:T(8,128)S(1)}, f32[48,16,128]{2,1,0:T(8,128)}, u32[]{:S(2)}) copy-start(f32[48,16,128]{2,1,0:T(8,128)} %vel.1) | copy-start | bytes 1179652
  4.6 1.0 %copy-start.4 = (f32[48,16,128]{2,1,0:T(8,128)S(1)}, f32[48,16,128]{2,1,0:T(8,128)}, u32[]{:S(2)}) copy-start(f32[48,16,128]{2,1,0:T(8,128)} %cap_in.1) | copy-start | bytes 1179652
  5.6 1.0 %copy-start.5 = (f32[48,16,128]{2,1,0:T(8,128)S(1)}, f32[48,16,128]{2,1,0:T(8,128)}, u32[]{:S(2)}) copy-start(f32[48,16,128]{2,1,0:T(8,128)} %capstep_in.1) | copy-start | bytes 1179652
  6.6 0.7 %copy-start.6 = (s32[6,2,16]{2,1,0:T(2,128)S(1)}, s32[6,2,16]{2,1,0:T(2,128)}, u32[]{:S(2)}) copy-start(s32[6,2,16]{2,1,0:T(2,128)} %mask.1) | copy-start | bytes 2308
  7.3 0.7 %copy-start.7 = (s32[6,2,16]{2,1,0:T(2,128)S(1)}, s32[6,2,16]{2,1,0:T(2,128)}, u32[]{:S(2)}) copy-start(s32[6,2,16]{2,1,0:T(2,128)} %label.1) | copy-start | bytes 2308
  8.0 0.7 %copy-start.8 = (f32[4]{0:T(128)S(1)}, f32[4]{0:T(128)}, u32[]{:S(2)}) copy-start(f32[4]{0:T(128)} %class_weight.1) | copy-start | bytes 52

commit v2 on v1

--- a/solution.py
+++ b/solution.py
@@ -17,9 +17,10 @@
 
 
 def kernel(
-    conc, disp, step, vel, cap_in, capstep_in, mask, label, class_weight,
+    conc, disp, step, vel, cap_in, capstep_in, mask_in, label_in, class_weight,
     out_d, out_c,
     f_in, f_mid, f_sc, f_first,
+    mask, label, up_in, up_mid, up_sc, up_first, down_in, down_mid, down_sc, down_first,
     cap, capstep, ratio, rate1, rate2, part, res_d, res_c,
     ys_in, ys_mid, ys_sc, ys_first,
     yr_in, yr_mid, yr_sc, yr_first,
@@ -40,7 +41,7 @@
     loads = []
     for i, (src, dst) in enumerate((
         (conc, main(f_in.at[0])), (disp, main(f_in.at[1])), (step, main(f_in.at[2])),
-        (vel, main(f_in.at[3])), (cap_in, cap), (capstep_in, capstep),
+        (vel, main(f_in.at[3])), (cap_in, cap), (capstep_in, capstep), (mask_in, mask), (label_in, label),
     )):
         load = pltpu.make_async_copy(src, dst, load_sem.at[i])
         load.start()
@@ -134,19 +135,39 @@
     def center(fields, i, x):
         return fields[i, x + 1, TOP:TOP + ny, :]
 
-    def ends(zr, i, x):
-        return pltpu.roll(zr[0, i], nz - 1 - 2 * x, 1)
-
-    def z_up(v, end):
-        return jnp.where(last_lane, end, pltpu.roll(v, nz - 1, 1))
-
-    def z_down(v, end):
-        return jnp.where(first_lane, end, pltpu.roll(v, 1, 1))
-
-    def around(fields, i, x, v, zr):
-        end = ends(zr, i, x)
+    def shift(fields, up, down, k_up, k_down):
+        def one(x, carry):
+            for i in range(k_down):
+                v = center(fields, i, x)
+                down[i, x] = pltpu.roll(v, 1, 1)
+                if i < k_up:
+                    up[i, x] = pltpu.roll(v, nz - 1, 1)
+            return carry
+
+        lax.fori_loop(0, nx, one, 0, unroll=8)
+
+    def patch(zr, up, down, k_up, k_down):
+        def one(x, carry):
+            for i in range(k_down):
+                end = pltpu.roll(zr[0, i], nz - 1 - 2 * x, 1)
+                pltpu.store(down.at[i, x], end, mask=first_lane)
+                if i < k_up:
+                    pltpu.store(up.at[i, x], end, mask=last_lane)
+            return carry
+
+        lax.fori_loop(0, nx, one, 0, unroll=8)
+
+    def pack(fields, zs, k):
+        def one(x, planes):
+            return tuple(pack_column(p, center(fields, i, x), x) for i, p in enumerate(planes))
+
+        planes = lax.fori_loop(0, nx, one, (jnp.zeros((ny, nz), jnp.float32),) * k, unroll=8)
+        for i in range(k):
+            zs[i] = planes[i]
+
+    def around(fields, i, x, up, down):
         return [
-            z_up(v, end), z_down(v, end),
+            up[i, x], down[i, x],
             fields[i, x + 2, TOP:TOP + ny, :], fields[i, x, TOP:TOP + ny, :],
             fields[i, x + 1, TOP + 1:TOP + 1 + ny, :], fields[i, x + 1, TOP - 1:TOP - 1 + ny, :],
         ]
@@ -166,13 +187,20 @@
 
     blank = jnp.zeros((ny, nz), jnp.float32)
 
-    def pack_in(x, planes):
-        return tuple(pack_column(p, center(f_in, i, x), x) for i, p in enumerate(planes))
-
-    planes = lax.fori_loop(0, nx, pack_in, (blank,) * 4, unroll=4)
-    for i in range(4):
-        zs_in[i] = planes[i]
+    pack(f_in, zs_in, 4)
     start(pairs, 2)
+    shift(f_in, up_in, down_in, 3, 4)
+    for load in loads[4:]:
+        load.wait()
+
+    def prepare(x, carry):
+        inv = 1.0 / cap[x]
+        r = time_step * inv
+        ratio[x] = r
+        capstep[x] = r * inv * capstep[x]
+        return carry
+
+    lax.fori_loop(0, nx, prepare, 0, unroll=4)
 
     sx, sy, sz = mask.shape
     weight[...] = jnp.zeros(weight.shape, jnp.float32)
@@ -185,53 +213,49 @@
         lax.broadcasted_iota(jnp.int32, (nz, nz), 0) == lax.broadcasted_iota(jnp.int32, (nz, nz), 1) // VOXEL
     ).astype(jnp.float32)
     weight[...] = jnp.dot(weight[...], spread, precision=EXACT, preferred_element_type=jnp.float32)
-    for load in loads[4:]:
-        load.wait()
-
     finish(pairs)
     unpack(f_in, yr_in, zr_in, 3)
-
-    def first(x, planes):
+    patch(zr_in, up_in, down_in, 3, 4)
+
+    def first(x, carry):
         c, d, s, v = (center(f_in, i, x) for i in range(4))
-        cn = around(f_in, 0, x, c, zr_in)
-        dn = around(f_in, 1, x, d, zr_in)
-        sn = around(f_in, 2, x, s, zr_in)
-        v_down = z_down(v, ends(zr_in, 3, x))
+        cn = around(f_in, 0, x, up_in, down_in)
+        dn = around(f_in, 1, x, up_in, down_in)
+        sn = around(f_in, 2, x, up_in, down_in)
+        v_down = down_in[3, x]
         diff = [n - c for n in cn]
         g_d = total([(d + k) * q for k, q in zip(dn, diff)])
         g_s = total([(s + k) * q for k, q in zip(sn, diff)])
         rate = 0.5 * g_d + v_down * cn[1] - v * c
-        inv = 1.0 / cap[x]
-        r = time_step * inv
-        cs = r * inv * capstep[x]
+        r = ratio[x]
+        cs = capstep[x]
         later = c + r * rate
         tangent = 0.5 * r * g_s - cs * rate
-        ratio[x] = r
-        capstep[x] = cs
         rate1[x] = rate
         f_mid[0, x + 1, TOP:TOP + ny, :] = later
         f_mid[1, x + 1, TOP:TOP + ny, :] = tangent
-        return pack_column(planes[0], later, x), pack_column(planes[1], tangent, x)
-
-    planes = lax.fori_loop(0, nx, first, (blank,) * 2, unroll=2)
+        return carry
+
+    lax.fori_loop(0, nx, first, 0, unroll=4)
     pairs = copies(1, f_mid, ys_mid, yr_mid, zs_mid, zr_mid)
     pack_rows(f_mid, ys_mid, 2)
     start(pairs, 1)
     start(pairs, 0)
-    zs_mid[0] = planes[0]
-    zs_mid[1] = planes[1]
+    pack(f_mid, zs_mid, 2)
     start(pairs, 2)
+    shift(f_mid, up_mid, down_mid, 2, 2)
     finish(pairs)
     unpack(f_mid, yr_mid, zr_mid, 2)
+    patch(zr_mid, up_mid, down_mid, 2, 2)
 
     def second_at(x):
         l, t = (center(f_mid, i, x) for i in range(2))
         d, s, v = (center(f_in, i, x) for i in range(1, 4))
-        ln = around(f_mid, 0, x, l, zr_mid)
-        tn = around(f_mid, 1, x, t, zr_mid)
-        dn = around(f_in, 1, x, d, zr_in)
-        sn = around(f_in, 2, x, s, zr_in)
-        v_down = z_down(v, ends(zr_in, 3, x))
+        ln = around(f_mid, 0, x, up_mid, down_mid)
+        tn = around(f_mid, 1, x, up_mid, down_mid)
+        dn = around(f_in, 1, x, up_in, down_in)
+        sn = around(f_in, 2, x, up_in, down_in)
+        v_down = down_in[3, x]
         l_diff = [n - l for n in ln]
         kd = [d + k for k in dn]
         rate = 0.5 * total([k * q for k, q in zip(kd, l_diff)]) + v_down * ln[1] - v * l
@@ -243,7 +267,7 @@
         def one(i, acc):
             return acc + second_at(g * VOXEL + i)
 
-        acc = lax.fori_loop(0, VOXEL, one, blank, unroll=2)
+        acc = lax.fori_loop(0, VOXEL, one, blank, unroll=4)
         sums = jnp.concatenate(
             [jnp.sum(acc[j * VOXEL:(j + 1) * VOXEL], axis=0, keepdims=True) for j in range(sy)], axis=0)
         coarse[pl.ds(g * sy, sy), :] = sums
@@ -261,66 +285,70 @@
         return jnp.concatenate(
             [jnp.broadcast_to(coarse[pl.ds(g * sy + j, 1), :], (VOXEL, nz)) for j in range(sy)], axis=0)
 
-    def scale(x, plane):
+    def scale(x, carry):
         scaled = ratio[x] * source_at(x)
         f_sc[0, x + 1, TOP:TOP + ny, :] = scaled
-        return pack_column(plane, scaled, x)
-
-    plane = lax.fori_loop(0, nx, scale, blank, unroll=4)
+        return carry
+
+    lax.fori_loop(0, nx, scale, 0, unroll=8)
     pairs = copies(2, f_sc, ys_sc, yr_sc, zs_sc, zr_sc)
     pack_rows(f_sc, ys_sc, 1)
     start(pairs, 1)
     start(pairs, 0)
-    zs_sc[0] = plane
+    pack(f_sc, zs_sc, 1)
     start(pairs, 2)
+    shift(f_sc, up_sc, down_sc, 1, 1)
     finish(pairs)
     unpack(f_sc, yr_sc, zr_sc, 1)
-
-    def third(x, plane):
+    patch(zr_sc, up_sc, down_sc, 1, 1)
+
+    def third(x, carry):
         d, v = center(f_in, 1, x), center(f_in, 3, x)
         w = center(f_sc, 0, x)
-        dn = around(f_in, 1, x, d, zr_in)
-        wn = around(f_sc, 0, x, w, zr_sc)
+        dn = around(f_in, 1, x, up_in, down_in)
+        wn = around(f_sc, 0, x, up_sc, down_sc)
         g = total([(d + k) * (n - w) for k, n in zip(dn, wn)])
         earlier = source_at(x) + 0.5 * g + v * (wn[0] - w)
         r = ratio[x]
         one = r * earlier
         f_first[0, x + 1, TOP:TOP + ny, :] = one
-        return pack_column(plane, one, x)
-
-    plane = lax.fori_loop(0, nx, third, blank, unroll=2)
+        return carry
+
+    lax.fori_loop(0, nx, third, 0, unroll=4)
     pairs = copies(3, f_first, ys_first, yr_first, zs_first, zr_first)
     pack_rows(f_first, ys_first, 1)
     start(pairs, 1)
     start(pairs, 0)
-    zs_first[0] = plane
+    pack(f_first, zs_first, 1)
     start(pairs, 2)
+    shift(f_first, up_first, down_first, 1, 1)
 
     def fourth(x, carry):
         w = center(f_sc, 0, x)
         l = center(f_mid, 0, x)
         one = center(f_first, 0, x)
-        wn = around(f_sc, 0, x, w, zr_sc)
-        ln = around(f_mid, 0, x, l, zr_mid)
+        wn = around(f_sc, 0, x, up_sc, down_sc)
+        ln = around(f_mid, 0, x, up_mid, down_mid)
         part[x] = total([(w - m) * (n - l) for m, n in zip(wn, ln)])
         res_c[x] = -(w * rate2[x] + one * rate1[x]) * (ratio[x] * (1.0 / time_step))
         return carry
 
-    lax.fori_loop(0, nx, fourth, 0, unroll=2)
+    lax.fori_loop(0, nx, fourth, 0, unroll=4)
     store_c = pltpu.make_async_copy(res_c, out_c, out_sem.at[0])
     store_c.start()
     finish(pairs)
     unpack(f_first, yr_first, zr_first, 1)
+    patch(zr_first, up_first, down_first, 1, 1)
 
     def fifth(x, carry):
         one = center(f_first, 0, x)
         c = center(f_in, 0, x)
-        on = around(f_first, 0, x, one, zr_first)
-        cn = around(f_in, 0, x, c, zr_in)
+        on = around(f_first, 0, x, up_first, down_first)
+        cn = around(f_in, 0, x, up_in, down_in)
         res_d[x] = 0.5 * (part[x] + total([(one - m) * (n - c) for m, n in zip(on, cn)]))
         return carry
 
-    lax.fori_loop(0, nx, fifth, 0, unroll=2)
+    lax.fori_loop(0, nx, fifth, 0, unroll=4)
     store_d = pltpu.make_async_copy(res_d, out_d, out_sem.at[1])
     store_d.start()
     store_c.wait()
@@ -331,8 +359,7 @@
     nx, ny, nz = concentration.shape
     f32 = jnp.float32
     block = jax.ShapeDtypeStruct((nx, ny, nz), f32)
-    hbm = pl.BlockSpec(memory_space=pl.ANY)
-    vmem = pl.BlockSpec(memory_space=pltpu.VMEM)
+    hbm = pl.BlockSpec(memory_space=pltpu.HBM)
     smem = pl.BlockSpec(memory_space=pltpu.SMEM)
     whole = pltpu.VMEM((nx, ny, nz), f32)
     coarse_rows = -(-(nx // VOXEL) * (ny // VOXEL) // 8) * 8
@@ -341,19 +368,22 @@
     fields = (4, 2, 1, 1)
     scratch = (
         [pltpu.VMEM((k, nx + 2, ny + 2 * EDGE, nz), f32) for k in fields]
+        + [pltpu.VMEM(voxel_mask.shape, jnp.int32)] * 2
+        + [pltpu.VMEM((k, nx, ny, nz), f32) for k in fields]
+        + [pltpu.VMEM((k, nx, ny, nz), f32) for k in fields]
         + [whole] * 8
         + [pltpu.VMEM((2, k, nx, nz), f32) for k in per_phase]
         + [pltpu.VMEM((2, k, nx, nz), f32) for k in per_phase]
         + [pltpu.VMEM((k, ny, nz), f32) for k in z_phase]
         + [pltpu.VMEM((2, k, ny, nz), f32) for k in z_phase]
         + [pltpu.VMEM((coarse_rows, nz), f32)] * 2
-        + [pltpu.SemaphoreType.DMA((6,)), pltpu.SemaphoreType.DMA((2,))]
+        + [pltpu.SemaphoreType.DMA((8,)), pltpu.SemaphoreType.DMA((2,))]
         + [pltpu.SemaphoreType.DMA((24,))] * 2
     )
     return pl.pallas_call(
         kernel,
         out_shape=(block, block),
-        in_specs=[hbm] * 6 + [vmem, vmem, smem],
+        in_specs=[hbm] * 8 + [smem],
         out_specs=(hbm, hbm),
         scratch_shapes=scratch,
         compiler_params=pltpu.CompilerParams(

time: 46.3 us -> 36.6 us (0.79)
  Pallas kernels: 35.7 us -> 26 us
    pallas_call x1, Pallas kernels: 35.7 us -> 26 us  [shards(): pl.pallas_call(kernel, out_shape=(block, block), in_specs=[hbm] * 8 + [sm...]
where the time goes in v2:
time: 36.6 us; the launch traced here: 36.1 us
  Pallas kernels  26 us (71%)
  local copies, waits for them, and re-layouts  9.5 us (26%)
  between operations  0.66 us (2%)
    pallas_call x1, Pallas kernels, shards(): pl.pallas_call(kernel, out_shape=(block, block), in_specs=[hbm] * 8 + [sm...  26 us
    unnamed x20, local copies, waits for them, and re-layouts  9.5 us

profile of v2, /device:TPU:0, one launch (start us, length us, event | category | flops | bytes accessed | tf_op | source)
XLA Modules:
  0.0 36.1 jit_solution(8094097287136873991)
XLA Ops:
  0.6 0.0 copy-start
  0.6 1.0 %copy-done = f32[48,16,128]{2,1,0:T(8,128)S(1)} copy-done((f32[48,16,128]{2,1,0:T(8,128)S(1)}, f32[48,16,128]{2,1,0:T(8,128)}, u32[]{:S(2)}) %copy-start) | copy-done | bytes 393240
  1.6 0.0 copy-start.1
  1.6 1.0 %copy-done.1 = f32[48,16,128]{2,1,0:T(8,128)S(1)} copy-done((f32[48,16,128]{2,1,0:T(8,128)S(1)}, f32[48,16,128]{2,1,0:T(8,128)}, u32[]{:S(2)}) %copy-start.1) | copy-done | bytes 393240
  2.6 0.0 copy-start.2
  2.6 1.0 %copy-done.2 = f32[48,16,128]{2,1,0:T(8,128)S(1)} copy-done((f32[48,16,128]{2,1,0:T(8,128)S(1)}, f32[48,16,128]{2,1,0:T(8,128)}, u32[]{:S(2)}) %copy-start.2) | copy-done | bytes 393240
  3.6 0.0 copy-start.3
  3.6 1.0 %copy-done.3 = f32[48,16,128]{2,1,0:T(8,128)S(1)} copy-done((f32[48,16,128]{2,1,0:T(8,128)S(1)}, f32[48,16,128]{2,1,0:T(8,128)}, u32[]{:S(2)}) %copy-start.3) | copy-done | bytes 393240
  4.6 0.0 copy-start.4
  4.6 1.0 %copy-done.4 = f32[48,16,128]{2,1,0:T(8,128)S(1)} copy-done((f32[48,16,128]{2,1,0:T(8,128)S(1)}, f32[48,16,128]{2,1,0:T(8,128)}, u32[]{:S(2)}) %copy-start.4) | copy-done | bytes 393240
  5.6 0.0 copy-start.5
  5.6 1.0 %copy-done.5 = f32[48,16,128]{2,1,0:T(8,128)S(1)} copy-done((f32[48,16,128]{2,1,0:T(8,128)S(1)}, f32[48,16,128]{2,1,0:T(8,128)}, u32[]{:S(2)}) %copy-start.5) | copy-done | bytes 393240
  6.6 0.0 copy-start.6
  6.6 0.7 %copy-done.6 = s32[6,2,16]{2,1,0:T(2,128)S(1)} copy-done((s32[6,2,16]{2,1,0:T(2,128)S(1)}, s32[6,2,16]{2,1,0:T(2,128)}, u32[]{:S(2)}) %copy-start.6) | copy-done | bytes 792
  7.3 0.0 copy-start.7
  7.3 0.7 %copy-done.7 = s32[6,2,16]{2,1,0:T(2,128)S(1)} copy-done((s32[6,2,16]{2,1,0:T(2,128)S(1)}, s32[6,2,16]{2,1,0:T(2,128)}, u32[]{:S(2)}) %copy-start.7) | copy-done | bytes 792
  8.0 0.0 copy-start.8
  8.0 0.7 %copy-done.8 = f32[4]{0:T(128)S(1)} copy-done((f32[4]{0:T(128)S(1)}, f32[4]{0:T(128)}, u32[]{:S(2)}) %copy-start.8) | copy-done | bytes 40
  8.7 26.0 %shard_map.104 = (f32[48,16,128]{2,1,0:T(8,128)S(1)}, f32[48,16,128]{2,1,0:T(8,128)S(1)}) custom-call(f32[48,16,128]{2,1,0:T(8,128)S(1)} %copy-done, f32[48,16,128]{2,1,0:T(8,128)S(1)} %copy-done.1, f32[48,16,128]{2,1,0:T(8,128)S(1)} %copy-done.2, f32[48,16,128]{2,1,0:T(8,128)S(1)} %copy-done.3, f32[48,16,128]{2,1,0:T(8,128)S(1)} %copy-done.4, ...), custom_call_target="tpu_custom_call" | custom-call | tf_op jit(solution)/shard_map/pallas_call | solution.py:383
  34.6 0.7 %copy.13 = f32[48,16,128]{2,1,0:T(8,128)} copy(f32[48,16,128]{2,1,0:T(8,128)S(1)} %get-tuple-element.4) | data formatting | bytes 786432
  35.4 0.7 %copy.14 = f32[48,16,128]{2,1,0:T(8,128)} copy(f32[48,16,128]{2,1,0:T(8,128)S(1)} %get-tuple-element.5) | data formatting | bytes 786432
Async XLA Ops:
  0.6 1.0 %copy-start = (f32[48,16,128]{2,1,0:T(8,128)S(1)}, f32[48,16,128]{2,1,0:T(8,128)}, u32[]{:S(2)}) copy-start(f32[48,16,128]{2,1,0:T(8,128)} %conc.1) | copy-start | bytes 1179652
  1.6 1.0 %copy-start.1 = (f32[48,16,128]{2,1,0:T(8,128)S(1)}, f32[48,16,128]{2,1,0:T(8,128)}, u32[]{:S(2)}) copy-start(f32[48,16,128]{2,1,0:T(8,128)} %disp.1) | copy-start | bytes 1179652
  2.6 1.0 %copy-start.2 = (f32[48,16,128]{2,1,0:T(8,128)S(1)}, f32[48,16,128]{2,1,0:T(8,128)}, u32[]{:S(2)}) copy-start(f32[48,16,128]{2,1,0:T(8,128)} %step.1) | copy-start | bytes 1179652
  3.6 1.0 %copy-start.3 = (f32[48,16,128]{2,1,0:T(8,128)S(1)}, f32[48,16,128]{2,1,0:T(8,128)}, u32[]{:S(2)}) copy-start(f32[48,16,128]{2,1,0:T(8,128)} %vel.1) | copy-start | bytes 1179652
  4.6 1.0 %copy-start.4 = (f32[48,16,128]{2,1,0:T(8,128)S(1)}, f32[48,16,128]{2,1,0:T(8,128)}, u32[]{:S(2)}) copy-start(f32[48,16,128]{2,1,0:T(8,128)} %cap_in.1) | copy-start | bytes 1179652
  5.6 1.0 %copy-start.5 = (f32[48,16,128]{2,1,0:T(8,128)S(1)}, f32[48,16,128]{2,1,0:T(8,128)}, u32[]{:S(2)}) copy-start(f32[48,16,128]{2,1,0:T(8,128)} %capstep_in.1) | copy-start | bytes 1179652
  6.6 0.7 %copy-start.6 = (s32[6,2,16]{2,1,0:T(2,128)S(1)}, s32[6,2,16]{2,1,0:T(2,128)}, u32[]{:S(2)}) copy-start(s32[6,2,16]{2,1,0:T(2,128)} %mask_in.1) | copy-start | bytes 2308
  7.3 0.7 %copy-start.7 = (s32[6,2,16]{2,1,0:T(2,128)S(1)}, s32[6,2,16]{2,1,0:T(2,128)}, u32[]{:S(2)}) copy-start(s32[6,2,16]{2,1,0:T(2,128)} %label_in.1) | copy-start | bytes 2308
  8.0 0.7 %copy-start.8 = (f32[4]{0:T(128)S(1)}, f32[4]{0:T(128)}, u32[]{:S(2)}) copy-start(f32[4]{0:T(128)} %class_weight.1) | copy-start | bytes 52
